TPU v7x, 32 devices: a whole 2x2x4 slice. The times are simulated.
32 devices in a mesh: fsdp: 8 (over y, x, core), grp: 4 (over z).
Axes of the slice: x: 2, y: 2, z: 4, core: 2. Of those that a mesh axis runs over, the one named last changes fastest.
Arguments:
- q_up: bfloat16 [128, 128, 1536], P('grp', None, 'fsdp'), may hold values from -0.15625 to 0.15625
- k_up: bfloat16 [128, 128, 512], P('grp', None, 'fsdp'), may hold values from -0.25 to 0.25
- v_up: bfloat16 [128, 128, 512], P('grp', None, 'fsdp'), may hold values from -0.25 to 0.25
- queries: bfloat16 [512, 1536], P(('fsdp', 'grp')), may hold values from -6 to 6
- cache: bfloat16 [65536, 512], P(('fsdp', 'grp')), may hold values from -360 to 360
- positions: int32 [512], P(('fsdp', 'grp')), may hold values from 256 to 2047, as said below
Outputs:
- heads_out: bfloat16 [512, 16384], P(('fsdp', 'grp'))
Inputs may be any that keep to these rules, and one draw needn't show every extreme that they name: `positions`: each row reads its own device's cache block up to this entry; some row reads the whole block.
All inputs are finite; a program needn't handle non-finite values.
Results may differ from a plain program's by a relative error of at most 0.006.
The roundings to bfloat16 on the way count: a program that leaves them out, or rounds other values in their place, can miss the bound.
Values may be sent and summed in bfloat16 or wider, within the bound.
A program may use at most 128 MiB of HBM per device.

v0:
```python
import jax
import jax.numpy as jnp
from jax import lax
from jax.sharding import PartitionSpec as P

score_scale = 192.0 ** (-0.5)


def attend(q_abs, keys, row_pos):
    scores = (
        jnp.einsum("rhk,jk->rhj", q_abs, keys, preferred_element_type=jnp.float32) * score_scale
    )
    cache_index = jnp.arange(keys.shape[0], dtype=jnp.int32)
    visible = cache_index[None, :] <= row_pos[:, None]
    scores = jnp.where(visible[:, None, :], scores, jnp.float32(-1e30))
    row_max = jnp.max(scores, axis=-1, keepdims=True)
    weights = jnp.exp(scores - row_max)
    attention = (weights / jnp.sum(weights, axis=-1, keepdims=True)).astype(jnp.bfloat16)
    latent = jnp.einsum("rhj,jk->rhk", attention, keys, preferred_element_type=jnp.float32)
    return latent.astype(jnp.bfloat16)


def absorb_heads(query_rows, key_rows):
    return jnp.einsum(
        "hdq,hdk->hqk", query_rows, key_rows, preferred_element_type=jnp.float32
    ).astype(jnp.bfloat16)


def shards(q_up, k_up, v_up, queries, cache, positions):
    group_rows = lax.all_gather(queries, "grp", axis=0, tiled=True)
    own_query, own_key = (
        lax.all_to_all(q_up, "fsdp", split_axis=0, concat_axis=2, tiled=True),
        lax.all_to_all(k_up, "fsdp", split_axis=0, concat_axis=2, tiled=True),
    )
    own_blocks = absorb_heads(own_query, own_key)
    q_abs = jnp.einsum(
        "rq,hqk->rhk",
        group_rows,
        lax.all_gather(own_blocks, "fsdp", axis=0, tiled=True),
        preferred_element_type=jnp.float32,
    ).astype(jnp.bfloat16)
    row_queries = lax.all_to_all(q_abs, "grp", split_axis=0, concat_axis=1, tiled=True)
    latent = attend(row_queries, cache, positions)
    value_proj = lax.all_gather(v_up, "fsdp", axis=2, tiled=True)
    by_heads = lax.all_to_all(latent, "grp", split_axis=1, concat_axis=0, tiled=True)
    projected = jnp.einsum(
        "rhk,hdk->rhd", by_heads, value_proj, preferred_element_type=jnp.float32
    ).astype(jnp.bfloat16)
    result = lax.all_to_all(projected, "grp", split_axis=0, concat_axis=1, tiled=True)
    return result.reshape(result.shape[0], result.shape[1] * result.shape[2])


def solution(mesh):
    placed = (
        P("grp", None, "fsdp"),
        P("grp", None, "fsdp"),
        P("grp", None, "fsdp"),
        P(("fsdp", "grp"), None),
        P(("fsdp", "grp"), None),
        P(("fsdp", "grp")),
    )
    return jax.shard_map(
        shards, mesh=mesh, in_specs=placed, out_specs=P(("fsdp", "grp"), None), check_vma=False
    )
```

profile of v0, /device:TPU:3, one launch (start us, length us, event | category | flops | bytes accessed | tf_op | source)
XLA Modules:
  0.0 482.5 jit_solution(4623765856878858076)
XLA Ops:
  6.5 12.8 %all_to_all.87 = bf16[32,128,64]{1,2,0:T(8,128)(2,1)S(1)} all-to-all(bf16[32,128,64]{1,2,0:T(8,128)(2,1)} %param.7), channel_id=1, replica_groups=mesh['fsdp'=8,'grp'=4] {'fsdp'}, dimensions={0} | all-to-all | bytes 1048576 | tf_op jit(solution)/shard_map/all_to_all | solution.py:33
  19.3 5.9 %all-to-all-start = ((bf16[32,128,192]{1,2,0:T(8,128)(2,1)}), bf16[32,128,192]{1,2,0:T(8,128)(2,1)}, u32[]{:S(2)}, u32[]{:S(2)}) async-start(bf16[32,128,192]{1,2,0:T(8,128)(2,1)} %param.6), calls=%async_computation | async-start | bytes 3145728 | tf_op jit(solution)/shard_map/all_to_all | solution.py:32
  25.2 19.5 %all-to-all-done = bf16[32,128,192]{1,2,0:T(8,128)(2,1)} async-done(((bf16[32,128,192]{1,2,0:T(8,128)(2,1)}), bf16[32,128,192]{1,2,0:T(8,128)(2,1)}, u32[]{:S(2)}, u32[]{:S(2)}) %all-to-all-start) | async-done | bytes 1572896 | tf_op jit(solution)/shard_map/all_to_all | solution.py:32
  44.7 1.5 copy.19
  46.2 4.4 convolution_convert_fusion
  50.7 0.8 copy-done.1
  51.4 11.9 %all_gather.10 = bf16[64,1536]{1,0:T(8,128)(2,1)S(1)} all-gather(bf16[16,1536]{1,0:T(8,128)(2,1)S(1)} %copy-done.1), channel_id=1, replica_groups=mesh['fsdp'=8,'grp'=4] {'grp'}, dimensions={0}, use_global_device_ids=true | all-gather | bytes 245760 | tf_op jit(solution)/shard_map/all_gather | solution.py:30
  63.3 220.2 %all-gather.3.cloned.1.call-done = bf16[32,1536,512]{2,1,0:T(8,128)(2,1)} async-done(((bf16[4,1536,512]{2,1,0:T(8,128)(2,1)}), bf16[32,1536,512]{2,1,0:T(8,128)(2,1)}) %all-gather.3.cloned.1.call-update) | async-done | bytes 50331664 | tf_op jit(solution)/shard_map/all_gather | solution.py:39
  283.6 21.5 %convert_bitcast_fusion = bf16[64,32,512]{2,0,1:T(8,128)(2,1)} fusion(bf16[32,1536,512]{2,1,0:T(8,128)(2,1)} %all-gather.3.cloned.1.call-done, bf16[64,1536]{1,0:T(8,128)(2,1)S(1)} %all_gather.10), kind=kOutput, calls=%fused_computation.13 | convolution fusion | flops 3222274048 | bytes 52625408 | tf_op jit(solution)/shard_map/rq,hqk->rhk/dot_general | solution.py:36
  305.1 4.1 copy.22
  309.2 4.5 all-to-all-start.2
  313.9 0.5 all-gather.5.cloned.1.call-update
  314.6 47.1 %all-to-all-done.2 = bf16[64,32,512]{2,1,0:T(8,128)(2,1)} async-done(((bf16[64,32,512]{2,1,0:T(8,128)(2,1)}), bf16[64,32,512]{2,1,0:T(8,128)(2,1)}, u32[]{:S(2)}, u32[]{:S(2)}) %all-to-all-start.2) | async-done | bytes 2097184 | tf_op jit(solution)/shard_map/all_to_all | solution.py:42
  361.6 1.7 copy.23
  363.4 8.3 %fusion.7 = f32[16,128,2048]{2,1,0:T(8,128)} fusion(bf16[16,128,512]{2,1,0:T(8,128)(2,1)S(1)} %bitcast.48, bf16[2048,512]{1,0:T(8,128)(2,1)S(1)} %copy-done), kind=kOutput, calls=%fused_computation.11 | convolution fusion | flops 4294967296 | bytes 20971520 | tf_op jit(solution)/shard_map/rhk,jk->rhj/dot_general | solution.py:11
  371.7 19.1 %fusion.16 = (f32[16,128]{1,0:T(8,128)S(1)}, f32[16,128,2048]{2,1,0:T(8,128)}) fusion(f32[16,128,2048]{2,1,0:T(8,128)} %fusion.7, pred[16,2048]{1,0:T(8,128)(4,1)S(1)} %iota_compare_fusion), kind=kOutput, calls=%fused_computation.22 | output fusion | flops 25167872 | bytes 33595392 | tf_op jit(solution)/shard_map/sub | solution.py:17
  390.9 10.5 %fusion.9 = bf16[16,128,512]{2,1,0:T(8,128)(2,1)S(1)} fusion(bf16[2048,512]{1,0:T(8,128)(2,1)S(1)} %copy-done, f32[16,128,2048]{2,1,0:T(8,128)} %get-tuple-element.6, f32[16,128]{1,0:T(8,128)S(1)} %get-tuple-element.5), kind=kOutput, calls=%fused_computation.14 | convolution fusion | flops 4304404480 | bytes 20979712 | tf_op jit(solution)/shard_map/rhj,jk->rhk/dot_general | solution.py:19
  401.4 1.2 copy.24
  402.6 49.7 %all_to_all.88 = bf16[16,128,512]{2,0,1:T(8,128)(2,1)S(1)} all-to-all(bf16[16,128,512]{2,0,1:T(8,128)(2,1)S(1)} %copy.24), channel_id=1, replica_groups=mesh['fsdp'=8,'grp'=4] {'grp'}, dimensions={1} | all-to-all | bytes 4194304 | tf_op jit(solution)/shard_map/all_to_all | solution.py:45
  452.3 1.5 copy.25
  453.8 3.7 fusion.12
  457.5 0.3 copy.26
  457.9 16.5 %all_to_all.89 = bf16[64,32,128]{2,1,0:T(8,128)(2,1)S(1)} all-to-all(bf16[64,32,128]{2,1,0:T(8,128)(2,1)S(1)} %copy.26), channel_id=1, replica_groups=mesh['fsdp'=8,'grp'=4] {'grp'}, dimensions={0} | all-to-all | bytes 1048576 | tf_op jit(solution)/shard_map/all_to_all | solution.py:49
  474.5 1.1 copy.31
  (12 shorter events, 0.4 us)
Async XLA Ops:
  6.5 356.8 %copy-start = (bf16[2048,512]{1,0:T(8,128)(2,1)S(1)}, bf16[2048,512]{1,0:T(8,128)(2,1)}, u32[]{:S(2)}) copy-start(bf16[2048,512]{1,0:T(8,128)(2,1)} %param.10) | copy-start | bytes 6291460
  19.3 25.4 %all-to-all-start = ((bf16[32,128,192]{1,2,0:T(8,128)(2,1)}), bf16[32,128,192]{1,2,0:T(8,128)(2,1)}, u32[]{:S(2)}, u32[]{:S(2)}) async-start(bf16[32,128,192]{1,2,0:T(8,128)(2,1)} %param.6), calls=%async_computation | async-start | bytes 3145728 | tf_op jit(solution)/shard_map/all_to_all | solution.py:32
  25.2 258.4 %all-gather.3.cloned.1.call-start = ((), (), s32[]{:S(2)}) async-start(), calls=%async_computation.5 | async-start | bytes 56623104 | tf_op jit(solution)/shard_map/all_gather | solution.py:39
  50.6 0.8 copy-start.1
  305.1 9.3 %copy-start.2 = (s32[16]{0:T(128)S(1)}, s32[16]{0:T(128)}, u32[]{:S(2)}) copy-start(s32[16]{0:T(128)} %param.11) | copy-start | bytes 196
  309.2 52.4 %all-to-all-start.2 = ((bf16[64,32,512]{2,1,0:T(8,128)(2,1)}), bf16[64,32,512]{2,1,0:T(8,128)(2,1)}, u32[]{:S(2)}, u32[]{:S(2)}) async-start(bf16[64,32,512]{2,1,0:T(8,128)(2,1)} %copy.22), calls=%async_computation.2 | async-start | bytes 4194304 | tf_op jit(solution)/shard_map/all_to_all | solution.py:42
  313.7 140.2 %all-gather.5.cloned.1.call-start = ((), (), s32[]{:S(2)}) async-start(), calls=%async_computation.6 | async-start | bytes 4718592 | tf_op jit(solution)/shard_map/all_gather | solution.py:44
Sparse Core Ops, SparseCore 0:
  50.8 232.7 all-gather.2
  316.4 37.3 all-gather.4
where the time goes:
time: 486 us; the launch traced here: 482 us
  waiting for transfers between devices  287 us (59%)
  blocking collectives  90.9 us (19%)
  matrix products  48.5 us (10%)
  other arithmetic  19.2 us (4%)
  between operations  13.5 us (3%)
  local copies, waits for them, and re-layouts  12.4 us (3%)
  starting transfers between devices  10.5 us (2%)
    all_gather x1, waiting for transfers between devices, shards(): lax.all_gather(own_blocks, 'fsdp', axis=0, tiled=True)  220 us
    all_to_all x1, blocking collectives, shards(): lax.all_to_all(latent, 'grp', split_axis=1, concat_axis=0, tiled=True)  49.7 us
    all_to_all x1, waiting for transfers between devices, shards(): lax.all_to_all(q_abs, 'grp', split_axis=0, concat_axis=1, tiled=True)  47.1 us
    dot_general x1, matrix products, shards(): jnp.einsum('rq,hqk->rhk', group_rows, lax.all_gather(own_blocks, 'fsdp',...  21.5 us
    all_to_all x1, waiting for transfers between devices, shards(): lax.all_to_all(q_up, 'fsdp', split_axis=0, concat_axis=2, tiled=True)  19.5 us
    sub x1, other arithmetic, attend(): weights = jnp.exp(scores - row_max)  19.1 us
    all_to_all x1, blocking collectives, shards(): lax.all_to_all(projected, 'grp', split_axis=0, concat_axis=1, tiled=True)  16.5 us
    all_to_all x1, blocking collectives, shards(): lax.all_to_all(k_up, 'fsdp', split_axis=0, concat_axis=2, tiled=True)  12.8 us
  transfers between devices with their start and end apart: 4, of which 3 were waited for; matrix products, arithmetic and copies ran while one was open for 9% of the time, Pallas kernels for 0%

commit v1 on v0

v1 whole, which is shorter than its diff:
```python
import functools

import jax
import jax.numpy as jnp
from jax import lax
from jax.experimental import pallas as pl
from jax.experimental.pallas import tpu as pltpu
from jax.sharding import PartitionSpec as P

score_scale = 192.0 ** (-0.5)
ROW_BLOCK = 2


def attend_body(pos_ref, q_ref, cache_ref, out_ref):
    step = pl.program_id(0)
    rows, heads, rank = q_ref.shape
    entries = cache_ref.shape[0]
    index = lax.broadcasted_iota(jnp.int32, (heads, entries), 1)
    for r in range(rows):
        scores = lax.dot_general(
            q_ref[r],
            cache_ref[...],
            (((1,), (1,)), ((), ())),
            preferred_element_type=jnp.float32,
        )
        scores = scores * score_scale
        scores = jnp.where(index <= pos_ref[step * rows + r], scores, jnp.float32(-1e30))
        top = jnp.max(scores, axis=-1, keepdims=True)
        weights = jnp.exp(scores - top)
        total = jnp.sum(weights, axis=-1, keepdims=True)
        probs = (weights * (1.0 / total)).astype(jnp.bfloat16)
        out_ref[r] = jnp.dot(
            probs, cache_ref[...], preferred_element_type=jnp.float32
        ).astype(jnp.bfloat16)


def attend(q_abs, keys, row_pos):
    rows, heads, rank = q_abs.shape
    block = ROW_BLOCK if rows % ROW_BLOCK == 0 else 1
    spec = pl.BlockSpec((block, heads, rank), lambda i, pos: (i, 0, 0))
    return pl.pallas_call(
        attend_body,
        out_shape=jax.ShapeDtypeStruct(q_abs.shape, jnp.bfloat16),
        grid_spec=pltpu.PrefetchScalarGridSpec(
            num_scalar_prefetch=1,
            grid=(rows // block,),
            in_specs=[spec, pl.BlockSpec(keys.shape, lambda i, pos: (0, 0))],
            out_specs=spec,
        ),
        compiler_params=pltpu.CompilerParams(vmem_limit_bytes=40 << 20),
        cost_estimate=pl.CostEstimate(
            flops=4 * rows * heads * keys.shape[0] * rank,
            bytes_accessed=2 * (2 * q_abs.size + keys.size),
            transcendentals=rows * heads * keys.shape[0],
        ),
    )(row_pos, q_abs, keys)


def absorb_heads(query_rows, key_rows):
    return jnp.einsum(
        "hdq,hdk->hqk", query_rows, key_rows, preferred_element_type=jnp.float32
    ).astype(jnp.bfloat16)


def shards(n_fsdp, n_grp, q_up, k_up, v_up, queries, cache, positions):
    rows = queries.shape[0]
    all_rows = lax.all_gather(queries, ("fsdp", "grp"), axis=0, tiled=True)
    own_query, own_key = (
        lax.all_to_all(q_up, "fsdp", split_axis=0, concat_axis=2, tiled=True),
        lax.all_to_all(k_up, "fsdp", split_axis=0, concat_axis=2, tiled=True),
    )
    own_blocks = absorb_heads(own_query, own_key)
    own_heads, _, rank = own_blocks.shape
    q_abs = jnp.einsum(
        "rq,hqk->rhk", all_rows, own_blocks, preferred_element_type=jnp.float32
    ).astype(jnp.bfloat16)
    row_queries = lax.all_to_all(
        q_abs, ("fsdp", "grp"), split_axis=0, concat_axis=1, tiled=True
    )
    latent = attend(row_queries, cache, positions)
    value_proj = lax.all_gather(v_up, "fsdp", axis=2, tiled=True)
    latent = latent.reshape(rows, n_fsdp, n_grp, own_heads * rank)
    by_heads = lax.all_to_all(latent, "grp", split_axis=2, concat_axis=0, tiled=True)
    by_heads = by_heads.reshape(rows * n_grp, n_fsdp * own_heads, rank)
    projected = jnp.einsum(
        "rhk,hdk->rhd", by_heads, value_proj, preferred_element_type=jnp.float32
    ).astype(jnp.bfloat16)
    result = lax.all_to_all(projected, "grp", split_axis=0, concat_axis=1, tiled=True)
    return result.reshape(result.shape[0], result.shape[1] * result.shape[2])


def solution(mesh):
    placed = (
        P("grp", None, "fsdp"),
        P("grp", None, "fsdp"),
        P("grp", None, "fsdp"),
        P(("fsdp", "grp"), None),
        P(("fsdp", "grp"), None),
        P(("fsdp", "grp")),
    )
    return jax.shard_map(
        functools.partial(shards, mesh.shape["fsdp"], mesh.shape["grp"]),
        mesh=mesh,
        in_specs=placed,
        out_specs=P(("fsdp", "grp"), None),
        check_vma=False,
    )
```

time: 486 us -> 255 us (0.52)
  waiting for transfers between devices: 287 us -> 91.8 us
  matrix products: 48.5 us -> 11.7 us
  Pallas kernels: 0 us -> 23.4 us
  other arithmetic: 19.2 us -> 0 us
  blocking collectives: 90.9 us -> 80.9 us
  local copies, waits for them, and re-layouts: 12.4 us -> 22.1 us
    all_gather x1, waiting for transfers between devices: 220 us -> 22.4 us  [shards(): all_rows = lax.all_gather(queries, ('fsdp', 'grp'), axis=0, tiled=True)]
    dot_general x4 -> x1, matrix products: 44.8 us -> 6.96 us  [shards(): jnp.einsum('rq,hqk->rhk', all_rows, own_blocks, preferred_element_type=jn...]
    pallas_call x0 -> x1, Pallas kernels: none -> 23.4 us  [attend(): pl.pallas_call(attend_body, out_shape=jax.ShapeDtypeStruct(q_abs.shape, j...]
    sub x1 -> x0, other arithmetic: 19.1 us -> none  [attend(): weights = jnp.exp(scores - row_max)]
    all_gather x1 -> x0, blocking collectives: 11.9 us -> none  [shards(): group_rows = lax.all_gather(queries, 'grp', axis=0, tiled=True)]
    reshape x0 -> x3, local copies, waits for them, and re-layouts: none -> 7.4 us  [the longest x2 4.3 us: shards(): latent = latent.reshape(rows, n_fsdp, n_grp, own_heads * rank)]
  transfers between devices with their start and end apart: 4 -> 4, of which waited for: 3 -> 3; matrix products, arithmetic and copies ran while one was open for 9% -> 5% of each run, Pallas kernels for 0% -> 9%
where the time goes in v1:
time: 255 us; the launch traced here: 254 us
  waiting for transfers between devices  91.8 us (36%)
  blocking collectives  80.9 us (32%)
  Pallas kernels  23.4 us (9%)
  local copies, waits for them, and re-layouts  22.1 us (9%)
  between operations  15 us (6%)
  matrix products  11.7 us (5%)
  starting transfers between devices  9.1 us (4%)
    all_to_all x1, blocking collectives, shards(): lax.all_to_all(latent, 'grp', split_axis=2, concat_axis=0, tiled=True)  51.7 us
    all_to_all x1, waiting for transfers between devices, shards(): lax.all_to_all(q_abs, ('fsdp', 'grp'), split_axis=0, concat_axis=1, tiled...  48.2 us
    pallas_call x1, Pallas kernels, attend(): pl.pallas_call(attend_body, out_shape=jax.ShapeDtypeStruct(q_abs.shape, j...  23.4 us
    all_gather x1, waiting for transfers between devices, shards(): all_rows = lax.all_gather(queries, ('fsdp', 'grp'), axis=0, tiled=True)  22.4 us
    all_to_all x1, waiting for transfers between devices, shards(): lax.all_to_all(q_up, 'fsdp', split_axis=0, concat_axis=2, tiled=True)  20.2 us
    all_to_all x1, blocking collectives, shards(): lax.all_to_all(projected, 'grp', split_axis=0, concat_axis=1, tiled=True)  16.6 us
    all_to_all x1, blocking collectives, shards(): lax.all_to_all(k_up, 'fsdp', split_axis=0, concat_axis=2, tiled=True)  12.6 us
    dot_general x1, matrix products, shards(): jnp.einsum('rq,hqk->rhk', all_rows, own_blocks, preferred_element_type=jn...  6.96 us
  transfers between devices with their start and end apart: 4, of which 3 were waited for; matrix products, arithmetic and copies ran while one was open for 5% of the time, Pallas kernels for 9%

profile of v1, /device:TPU:3, one launch (start us, length us, event | category | flops | bytes accessed | tf_op | source)
XLA Modules:
  0.0 254.0 jit_solution(7859556474550320755)
XLA Ops:
  7.4 0.7 all-gather.3.cloned.1.call-update
  8.1 12.6 %all_to_all.84 = bf16[32,128,64]{1,2,0:T(8,128)(2,1)S(1)} all-to-all(bf16[32,128,64]{1,2,0:T(8,128)(2,1)} %param.7), channel_id=1, replica_groups=mesh['fsdp'=8,'grp'=4] {'fsdp'}, dimensions={0} | all-to-all | bytes 1048576 | tf_op jit(solution)/shard_map/all_to_all | solution.py:70
  20.7 5.2 %all-to-all-start = ((bf16[32,128,192]{1,2,0:T(8,128)(2,1)}), bf16[32,128,192]{1,2,0:T(8,128)(2,1)S(1)}, u32[]{:S(2)}, u32[]{:S(2)}) async-start(bf16[32,128,192]{1,2,0:T(8,128)(2,1)} %param.6), calls=%async_computation | async-start | bytes 3145728 | tf_op jit(solution)/shard_map/all_to_all | solution.py:69
  25.9 20.2 %all-to-all-done = bf16[32,128,192]{1,2,0:T(8,128)(2,1)S(1)} async-done(((bf16[32,128,192]{1,2,0:T(8,128)(2,1)}), bf16[32,128,192]{1,2,0:T(8,128)(2,1)S(1)}, u32[]{:S(2)}, u32[]{:S(2)}) %all-to-all-start) | async-done | bytes 1572896 | tf_op jit(solution)/shard_map/all_to_all | solution.py:69
  46.2 1.3 copy.23
  47.4 22.4 %all-gather.3.cloned.1.call-done = bf16[512,1536]{1,0:T(8,128)(2,1)} async-done(((bf16[16,1536]{1,0:T(8,128)(2,1)}), bf16[512,1536]{1,0:T(8,128)(2,1)}) %all-gather.3.cloned.1.call-update) | async-done | bytes 1572880 | tf_op jit(solution)/shard_map/all_gather | solution.py:67
  69.8 7.0 %convert_bitcast_fusion = bf16[512,4,512]{0,2,1:T(8,128)(2,1)S(1)} fusion(bf16[4,128,1536]{1,2,0:T(8,128)(2,1)} %bitcast.42, bf16[4,128,512]{1,2,0:T(8,128)(2,1)S(1)} %bitcast.43, bf16[512,1536]{1,0:T(8,128)(2,1)} %all-gather.3.cloned.1.call-done), kind=kOutput, calls=%fused_computation.5 | convolution fusion | flops 4030726144 | bytes 5767168 | tf_op jit(solution)/shard_map/rq,hqk->rhk/dot_general | solution.py:74
  76.8 3.1 %copy.27 = bf16[512,4,512]{2,1,0:T(4,128)(2,1)} copy(bf16[512,4,512]{0,2,1:T(8,128)(2,1)S(1)} %convert_bitcast_fusion) | data formatting | bytes 4194304 | tf_op jit(solution)/shard_map/convert_element_type | solution.py:76
  79.8 3.7 %all-to-all-start.2 = ((bf16[512,4,512]{2,1,0:T(4,128)(2,1)}), bf16[512,4,512]{2,1,0:T(4,128)(2,1)S(1)}, u32[]{:S(2)}, u32[]{:S(2)}) async-start(bf16[512,4,512]{2,1,0:T(4,128)(2,1)} %copy.27), calls=%async_computation.2 | async-start | bytes 4194304 | tf_op jit(solution)/shard_map/all_to_all | solution.py:77
  84.1 48.2 %all-to-all-done.2 = bf16[512,4,512]{2,1,0:T(4,128)(2,1)S(1)} async-done(((bf16[512,4,512]{2,1,0:T(4,128)(2,1)}), bf16[512,4,512]{2,1,0:T(4,128)(2,1)S(1)}, u32[]{:S(2)}, u32[]{:S(2)}) %all-to-all-start.2) | async-done | bytes 2097184 | tf_op jit(solution)/shard_map/all_to_all | solution.py:77
  132.3 0.4 copy.28
  132.7 2.9 %copy.29 = bf16[16,32,4,512]{3,2,1,0:T(4,128)(2,1)} copy(bf16[16,32,4,512]{3,0,1,2:T(8,128)(2,1)S(1)} %bitcast.36) | data formatting | bytes 4194304 | tf_op jit(solution)/shard_map/all_to_all | solution.py:77
  135.7 2.6 %all_to_all.72.q_ref = bf16[16,128,512]{2,1,0:T(8,128)(2,1)S(1)} reshape(bf16[16,32,4,512]{3,2,1,0:T(4,128)(2,1)} %copy.29) | data formatting | bytes 4194304 | tf_op jit(solution)/shard_map/all_to_all | solution.py:77
  138.2 1.6 copy-done.1
  139.8 23.4 %shard_map.64 = bf16[16,128,512]{2,1,0:T(8,128)(2,1)S(1)} custom-call(s32[16]{0:T(128)S(1)} %copy-done.2, bf16[16,128,512]{2,1,0:T(8,128)(2,1)S(1)} %all_to_all.72.q_ref, bf16[2048,512]{1,0:T(8,128)(2,1)S(1)} %copy-done.1), custom_call_target="tpu_custom_call" | custom-call | flops 8589934592 | bytes 6291456 | tf_op jit(solution)/shard_map/pallas_call | solution.py:41
  163.3 1.3 copy-done
  164.6 3.1 %reshape.11 = bf16[16,8,4,2048]{3,2,1,0:T(4,128)(2,1)S(1)} reshape(bf16[16,128,512]{2,1,0:T(8,128)(2,1)} %copy-done) | data formatting | bytes 4194304 | tf_op jit(solution)/shard_map/reshape | solution.py:82
  167.7 1.2 copy.30
  168.9 51.7 %all_to_all.85 = bf16[16,8,4,2048]{3,1,0,2:T(8,128)(2,1)} all-to-all(bf16[16,8,4,2048]{3,1,0,2:T(8,128)(2,1)S(1)} %copy.30), channel_id=1, replica_groups=mesh['fsdp'=8,'grp'=4] {'grp'}, dimensions={2} | all-to-all | bytes 4194304 | tf_op jit(solution)/shard_map/all_to_all | solution.py:83
  220.6 3.1 %reshape.12 = bf16[64,32,512]{2,1,0:T(8,128)(2,1)S(1)} reshape(bf16[4,16,8,1,2048]{4,2,1,0,3:T(8,128)(2,1)} %bitcast.37) | data formatting | bytes 4194304 | tf_op jit(solution)/shard_map/reshape | solution.py:84
  223.7 4.7 %fusion.12 = bf16[64,32,128]{2,0,1:T(8,128)(2,1)S(1)} fusion(bf16[32,128,512]{1,2,0:T(8,128)(2,1)} %all-gather.5.cloned.1.call-done, bf16[64,32,512]{2,1,0:T(8,128)(2,1)S(1)} %reshape.12), kind=kOutput, calls=%fused_computation.8 | convolution fusion | flops 268697600 | bytes 6815744 | tf_op jit(solution)/shard_map/rhk,hdk->rhd/dot_general | solution.py:85
  228.4 0.3 copy.32
  228.8 16.6 %all_to_all.86 = bf16[64,32,128]{2,1,0:T(8,128)(2,1)S(1)} all-to-all(bf16[64,32,128]{2,1,0:T(8,128)(2,1)S(1)} %copy.32), channel_id=1, replica_groups=mesh['fsdp'=8,'grp'=4] {'grp'}, dimensions={0} | all-to-all | bytes 1048576 | tf_op jit(solution)/shard_map/all_to_all | solution.py:88
  245.4 1.1 copy.44
  (10 shorter events, 0.7 us)
Async XLA Ops:
  7.4 62.4 %all-gather.3.cloned.1.call-start = ((), (), s32[]{:S(2)}) async-start(), calls=%async_computation.5 | async-start | bytes 1622016 | tf_op jit(solution)/shard_map/all_gather | solution.py:67
  20.7 25.4 %all-to-all-start = ((bf16[32,128,192]{1,2,0:T(8,128)(2,1)}), bf16[32,128,192]{1,2,0:T(8,128)(2,1)S(1)}, u32[]{:S(2)}, u32[]{:S(2)}) async-start(bf16[32,128,192]{1,2,0:T(8,128)(2,1)} %param.6), calls=%async_computation | async-start | bytes 3145728 | tf_op jit(solution)/shard_map/all_to_all | solution.py:69
  79.8 52.5 %all-to-all-start.2 = ((bf16[512,4,512]{2,1,0:T(4,128)(2,1)}), bf16[512,4,512]{2,1,0:T(4,128)(2,1)S(1)}, u32[]{:S(2)}, u32[]{:S(2)}) async-start(bf16[512,4,512]{2,1,0:T(4,128)(2,1)} %copy.27), calls=%async_computation.2 | async-start | bytes 4194304 | tf_op jit(solution)/shard_map/all_to_all | solution.py:77
  83.5 140.2 %all-gather.5.cloned.1.call-start = ((), (), s32[]{:S(2)}) async-start(), calls=%async_computation.6 | async-start | bytes 4718592 | tf_op jit(solution)/shard_map/all_gather | solution.py:81
  135.6 2.6 %copy-start.2 = (s32[16]{0:T(128)S(1)}, s32[16]{0:T(128)}, u32[]{:S(2)}) copy-start(s32[16]{0:T(128)} %pos_ref.1) | copy-start | bytes 196
  138.2 1.6 copy-start.1
  163.2 1.3 copy-start
Sparse Core Ops, SparseCore 0:
  11.1 58.6 all-gather.2
Sparse Core Ops, SparseCore 1:
  85.9 50.0 all-gather.4

commit v2 on v0

v2 whole, which is shorter than its diff:
```python
import functools

import jax
import jax.numpy as jnp
from jax import lax
from jax.experimental import pallas as pl
from jax.experimental.pallas import tpu as pltpu
from jax.sharding import PartitionSpec as P

score_scale = 192.0 ** (-0.5)
VMEM = 50 << 20


def front_body(
    n_fsdp,
    n_grp,
    q_cols,
    qk_ref,
    queries_ref,
    out_ref,
    qk_all,
    rows_all,
    absorbed,
    local_sem,
    qk_send,
    qk_recv,
    grp_send,
    grp_recv,
    far_send,
    far_recv,
    pair_send,
    pair_recv,
):
    f, g = lax.axis_index("fsdp"), lax.axis_index("grp")
    pairs = n_fsdp // 2
    chip, core = lax.div(f, 2), lax.rem(f, 2)
    partner = chip * 2 + 1 - core

    def send(src, dst, sems, slot, target):
        return pltpu.make_async_remote_copy(
            src_ref=src,
            dst_ref=dst,
            send_sem=sems[0].at[target[2]],
            recv_sem=sems[1].at[slot],
            device_id=(target[0], target[1]),
            device_id_type=pl.DeviceIdType.MESH,
        )

    barrier = pltpu.get_barrier_semaphore()

    @pl.loop(1, n_fsdp)
    def _(step):
        pl.semaphore_signal(
            barrier,
            inc=1,
            device_id=(lax.rem(f + step, n_fsdp), g),
            device_id_type=pl.DeviceIdType.MESH,
        )

    @pl.loop(1, n_grp)
    def _(step):
        pl.semaphore_signal(
            barrier,
            inc=1,
            device_id=(f, lax.rem(g + step, n_grp)),
            device_id_type=pl.DeviceIdType.MESH,
        )

    own_qk = pltpu.make_async_copy(qk_ref.at[f], qk_all.at[f], local_sem.at[0])
    own_rows = pltpu.make_async_copy(queries_ref, rows_all.at[f, g], local_sem.at[1])
    own_qk.start()
    own_rows.start()
    pl.semaphore_wait(barrier, n_fsdp + n_grp - 2)

    def grp_copy(peer, slot):
        return send(
            queries_ref, rows_all.at[f, slot], (grp_send, grp_recv), slot, (f, peer, peer)
        )

    def qk_copy(peer, slot):
        return send(
            qk_ref.at[peer], qk_all.at[slot], (qk_send, qk_recv), slot, (peer, g, peer)
        )

    def far_copy(peer, slot):
        return send(
            rows_all.at[slot], rows_all.at[slot], (far_send, far_recv), slot, (peer, g, peer)
        )

    def pair_copy(slot):
        return send(
            rows_all.at[slot],
            rows_all.at[slot],
            (pair_send, pair_recv),
            lax.div(slot, 2),
            (partner, g, lax.div(slot, 2)),
        )

    @pl.loop(1, n_grp)
    def _(step):
        grp_copy(lax.rem(g + step, n_grp), g).start()

    @pl.loop(1, n_fsdp)
    def _(step):
        qk_copy(lax.rem(f + step, n_fsdp), f).start()

    own_rows.wait()

    @pl.loop(1, n_grp)
    def _(step):
        other = lax.rem(g + step, n_grp)
        grp_copy(other, other).wait_recv()

    @pl.loop(1, pairs)
    def _(step):
        far_copy(lax.rem(chip + step, pairs) * 2 + core, f).start()

    pair_copy(f).start()

    @pl.loop(1, pairs)
    def _(step):
        other = lax.rem(chip + step, pairs) * 2 + core
        far_copy(other, other).wait_recv()
        pair_copy(other).start()

    own_qk.wait()

    @pl.loop(1, n_fsdp)
    def _(step):
        other = lax.rem(f + step, n_fsdp)
        qk_copy(other, other).wait_recv()

    heads = qk_all.shape[1]

    @pl.loop(0, heads)
    def _(h):
        keys = jnp.concatenate([qk_all[s, h, :, q_cols:] for s in range(n_fsdp)], axis=-1)
        for s in range(n_fsdp):
            absorbed[h, s * q_cols : (s + 1) * q_cols, :] = lax.dot_general(
                qk_all[s, h, :, :q_cols],
                keys,
                (((0,), (0,)), ((), ())),
                preferred_element_type=jnp.float32,
            ).astype(jnp.bfloat16)

    @pl.loop(0, pairs)
    def _(step):
        pair_copy(step * 2 + 1 - core).wait_recv()

    devices, _, rows, rank = out_ref.shape

    @pl.loop(0, heads)
    def _(h):
        @pl.loop(0, n_fsdp)
        def _(s):
            block = rows_all[s].reshape(n_grp * rows, rows_all.shape[-1])
            q_abs = jnp.dot(block, absorbed[h], preferred_element_type=jnp.float32)
            out_ref[pl.ds(s * n_grp, n_grp), h] = q_abs.astype(jnp.bfloat16).reshape(
                n_grp, rows, rank
            )

    @pl.loop(1, n_grp)
    def _(step):
        grp_copy(lax.rem(g + step, n_grp), g).wait_send()

    @pl.loop(1, n_fsdp)
    def _(step):
        qk_copy(lax.rem(f + step, n_fsdp), f).wait_send()

    @pl.loop(1, pairs)
    def _(step):
        far_copy(lax.rem(chip + step, pairs) * 2 + core, f).wait_send()

    @pl.loop(0, pairs)
    def _(step):
        pair_copy(step * 2 + core).wait_send()


def absorbed_queries(n_fsdp, n_grp, qk, queries, q_cols):
    _, heads, hd, cols = qk.shape
    rows, q_rank = queries.shape
    rank = n_fsdp * (cols - q_cols)
    devices = n_fsdp * n_grp
    dma = pltpu.SemaphoreType.DMA
    return pl.pallas_call(
        functools.partial(front_body, n_fsdp, n_grp, q_cols),
        out_shape=jax.ShapeDtypeStruct((devices, heads, rows, rank), jnp.bfloat16),
        in_specs=[pl.BlockSpec(memory_space=pl.ANY)] * 2,
        out_specs=pl.BlockSpec(memory_space=pltpu.VMEM),
        scratch_shapes=[
            pltpu.VMEM((n_fsdp, heads, hd, cols), jnp.bfloat16),
            pltpu.VMEM((n_fsdp, n_grp, rows, q_rank), jnp.bfloat16),
            pltpu.VMEM((heads, q_rank, rank), jnp.bfloat16),
            dma((2,)),
            dma((n_fsdp,)),
            dma((n_fsdp,)),
            dma((n_grp,)),
            dma((n_grp,)),
            dma((n_fsdp,)),
            dma((n_fsdp,)),
            dma((n_fsdp // 2,)),
            dma((n_fsdp // 2,)),
        ],
        compiler_params=pltpu.CompilerParams(
            vmem_limit_bytes=VMEM, collective_id=0, has_side_effects=True
        ),
        cost_estimate=pl.CostEstimate(
            flops=2 * heads * q_rank * rank * (hd + rows * devices),
            bytes_accessed=2 * (qk.size + heads * rows * devices * rank),
            transcendentals=0,
        ),
    )(qk, queries)


def attend_body(pos_ref, q_ref, cache_ref, out_ref):
    block = q_ref.shape
    q = q_ref[...].reshape(-1, block[-1])
    entries = cache_ref.shape[0]
    index = lax.broadcasted_iota(jnp.int32, (q.shape[0], entries), 1)
    scores = lax.dot_general(
        q, cache_ref[...], (((1,), (1,)), ((), ())), preferred_element_type=jnp.float32
    )
    scores = jnp.where(index <= pos_ref[...], scores * score_scale, jnp.float32(-1e30))
    top = jnp.max(scores, axis=-1, keepdims=True)
    weights = jnp.exp(scores - top)
    total = jnp.sum(weights, axis=-1, keepdims=True)
    probs = (weights * (1.0 / total)).astype(jnp.bfloat16)
    latent = jnp.dot(probs, cache_ref[...], preferred_element_type=jnp.float32)
    out_ref[...] = latent.astype(jnp.bfloat16).reshape(block)


def attend(q_abs, keys, row_pos, per_step):
    devices, heads, rows, rank = q_abs.shape
    pos = jnp.tile(row_pos, per_step * heads)[:, None]
    spec = pl.BlockSpec((per_step, heads, rows, rank), lambda i: (i, 0, 0, 0))
    return pl.pallas_call(
        attend_body,
        out_shape=jax.ShapeDtypeStruct(q_abs.shape, jnp.bfloat16),
        grid=(devices // per_step,),
        in_specs=[
            pl.BlockSpec(pos.shape, lambda i: (0, 0)),
            spec,
            pl.BlockSpec(keys.shape, lambda i: (0, 0)),
        ],
        out_specs=spec,
        compiler_params=pltpu.CompilerParams(vmem_limit_bytes=VMEM),
        cost_estimate=pl.CostEstimate(
            flops=4 * q_abs.size * keys.shape[0],
            bytes_accessed=2 * (2 * q_abs.size + keys.size),
            transcendentals=q_abs.size // rank * keys.shape[0],
        ),
    )(pos, q_abs, keys)


def project_body(latent_ref, value_ref, out_ref):
    n_f, _, per, rows, rank = latent_ref.shape
    hd = value_ref.shape[-1]
    for f in range(n_f):
        for i in range(per):
            h = f * per + i
            out_ref[:, h * hd : (h + 1) * hd] = jnp.dot(
                latent_ref[f, 0, i],
                value_ref[:, 0, h].reshape(rank, hd),
                preferred_element_type=jnp.float32,
            ).astype(jnp.bfloat16)


def project(latent, values, f_step):
    n_f, n_g, per, rows, rank = latent.shape
    _, _, heads, cols, hd = values.shape
    steps = n_f // f_step
    return pl.pallas_call(
        project_body,
        out_shape=jax.ShapeDtypeStruct((rows, n_g * heads * hd), jnp.bfloat16),
        grid=(n_g, steps),
        in_specs=[
            pl.BlockSpec((f_step, 1, per, rows, rank), lambda g, s: (s, g, 0, 0, 0)),
            pl.BlockSpec((n_f, 1, f_step * per, cols, hd), lambda g, s: (0, g, s, 0, 0)),
        ],
        out_specs=pl.BlockSpec((rows, f_step * per * hd), lambda g, s: (0, g * steps + s)),
        compiler_params=pltpu.CompilerParams(vmem_limit_bytes=VMEM),
        cost_estimate=pl.CostEstimate(
            flops=2 * latent.size * hd,
            bytes_accessed=2 * (latent.size + values.size),
            transcendentals=0,
        ),
    )(latent, values)


def shards(n_fsdp, n_grp, q_up, k_up, v_up, queries, cache, positions):
    heads, hd, q_cols = q_up.shape
    own = heads // n_fsdp
    qk = jnp.concatenate([q_up, k_up], axis=-1)
    qk = qk.reshape(n_fsdp, own, hd, qk.shape[-1])
    values = lax.all_gather(jnp.swapaxes(v_up, 1, 2), ("fsdp", "grp"), axis=0)
    values = values.reshape(n_fsdp, n_grp, *values.shape[1:])
    q_abs = absorbed_queries(n_fsdp, n_grp, qk, queries, q_cols)
    row_queries = lax.all_to_all(q_abs, ("fsdp", "grp"), split_axis=0, concat_axis=0)
    latent = attend(row_queries, cache, positions, max(1, 16 // own))
    latent = latent.reshape(n_fsdp, n_grp, *latent.shape[1:])
    return project(latent, values, max(1, min(n_fsdp, 16 // own)))


def solution(mesh):
    placed = (
        P("grp", None, "fsdp"),
        P("grp", None, "fsdp"),
        P("grp", None, "fsdp"),
        P(("fsdp", "grp"), None),
        P(("fsdp", "grp"), None),
        P(("fsdp", "grp")),
    )
    return jax.shard_map(
        functools.partial(shards, mesh.shape["fsdp"], mesh.shape["grp"]),
        mesh=mesh,
        in_specs=placed,
        out_specs=P(("fsdp", "grp"), None),
        check_vma=False,
    )
```

time: 486 us -> 201 us (0.41)
  waiting for transfers between devices: 287 us -> 90.1 us
  blocking collectives: 90.9 us -> 0 us
  Pallas kernels: 0 us -> 86.7 us
  matrix products: 48.5 us -> 0 us
  other arithmetic: 19.2 us -> 1.76 us
  local copies, waits for them, and re-layouts: 12.4 us -> 3.06 us
  starting transfers between devices: 10.5 us -> 4.39 us
    all_gather x2 -> x1, waiting for transfers between devices: 220 us -> 0.02 us  [shards(): values = lax.all_gather(jnp.swapaxes(v_up, 1, 2), ('fsdp', 'grp'), axis=0)]
    pallas_call x0 -> x3, Pallas kernels: none -> 86.7 us  [the longest x1 59.9 us: absorbed_queries(): pl.pallas_call(functools.partial(front_body, n_fsdp, n_grp, q_cols), out_...]
    all_to_all x3 -> x0, blocking collectives: 79 us -> none  [the longest x1 49.7 us: shards(): lax.all_to_all(latent, 'grp', split_axis=1, concat_axis=0, tiled=True)]
    dot_general x5 -> x0, matrix products: 48.5 us -> none  [the longest x1 21.5 us: shards(): jnp.einsum('rq,hqk->rhk', group_rows, lax.all_gather(own_blocks, 'fsdp',...]
    all_to_all x2 -> x1, waiting for transfers between devices: 66.6 us -> 89.4 us  [shards(): lax.all_to_all(q_abs, ('fsdp', 'grp'), split_axis=0, concat_axis=0)]
    sub x1 -> x0, other arithmetic: 19.1 us -> none  [attend(): weights = jnp.exp(scores - row_max)]
    all_gather x1 -> x0, blocking collectives: 11.9 us -> none  [shards(): group_rows = lax.all_gather(queries, 'grp', axis=0, tiled=True)]
    all_to_all x2 -> x1, starting transfers between devices: 10.3 us -> 4.39 us  [shards(): lax.all_to_all(q_abs, ('fsdp', 'grp'), split_axis=0, concat_axis=0)]
  transfers between devices with their start and end apart: 4 -> 2, of which waited for: 3 -> 1; matrix products, arithmetic and copies ran while one was open for 9% -> 2% of each run, Pallas kernels for 0% -> 39%
where the time goes in v2:
time: 201 us; the launch traced here: 200 us
  waiting for transfers between devices  90.1 us (45%)
  Pallas kernels  86.7 us (43%)
  between operations  13.5 us (7%)
  starting transfers between devices  4.39 us (2%)
  local copies, waits for them, and re-layouts  3.06 us (2%)
    all_to_all x1, waiting for transfers between devices, shards(): lax.all_to_all(q_abs, ('fsdp', 'grp'), split_axis=0, concat_axis=0)  89.4 us
    pallas_call x1, Pallas kernels, absorbed_queries(): pl.pallas_call(functools.partial(front_body, n_fsdp, n_grp, q_cols), out_...  59.9 us
    pallas_call x1, Pallas kernels, attend(): pl.pallas_call(attend_body, out_shape=jax.ShapeDtypeStruct(q_abs.shape, j...  17 us
    pallas_call x1, Pallas kernels, project(): pl.pallas_call(project_body, out_shape=jax.ShapeDtypeStruct((rows, n_g *...  9.85 us
    all_to_all x1, starting transfers between devices, shards(): lax.all_to_all(q_abs, ('fsdp', 'grp'), split_axis=0, concat_axis=0)  4.39 us
  transfers between devices with their start and end apart: 2, of which 1 were waited for; matrix products, arithmetic and copies ran while one was open for 2% of the time, Pallas kernels for 39%

profile of v2, /device:TPU:3, one launch (start us, length us, event | category | flops | bytes accessed | tf_op | source)
XLA Modules:
  0.0 199.6 jit_solution(17548570296407643716)
XLA Ops:
  6.5 0.0 all-gather.3.cloned.1.call-start
  6.5 0.7 all-gather.3.cloned.1.call-update
  7.3 1.8 pad_maximum_fusion
  9.0 0.0 copy-start
  9.0 2.9 %copy.10 = bf16[32,128,256]{2,1,0:T(8,128)(2,1)} copy(bf16[32,128,256]{1,2,0:T(8,128)(2,1)S(1)} %pad_maximum_fusion) | data formatting | bytes 4194304 | tf_op jit(solution)/shard_map/concatenate | solution.py:293
  12.0 0.0 copy-done
  12.0 59.9 %shard_map.64 = bf16[32,4,16,512]{3,2,1,0:T(8,128)(2,1)} custom-call(bf16[8,4,128,256]{3,2,1,0:T(8,128)(2,1)} %bitcast.6, bf16[16,1536]{1,0:T(8,128)(2,1)S(1)} %copy-done), custom_call_target="tpu_custom_call" | custom-call | flops 4026531840 | bytes 4194304 | tf_op jit(solution)/shard_map/pallas_call | solution.py:185
  71.9 0.0 copy-start.1
  71.9 4.4 %all-to-all-start = ((bf16[32,4,16,512]{3,2,1,0:T(8,128)(2,1)}), bf16[32,4,16,512]{3,2,1,0:T(8,128)(2,1)}, u32[]{:S(2)}, u32[]{:S(2)}) async-start(bf16[32,4,16,512]{3,2,1,0:T(8,128)(2,1)} %shard_map.64), calls=%async_computation | async-start | bytes 4194304 | tf_op jit(solution)/shard_map/all_to_all | solution.py:298
  76.3 0.0 copy-done.1
  76.3 0.1 broadcast_in_dim_tile.4.pos_ref
  76.4 89.4 %all-to-all-done.q_ref = bf16[32,4,16,512]{3,2,1,0:T(8,128)(2,1)} async-done(((bf16[32,4,16,512]{3,2,1,0:T(8,128)(2,1)}), bf16[32,4,16,512]{3,2,1,0:T(8,128)(2,1)}, u32[]{:S(2)}, u32[]{:S(2)}) %all-to-all-start) | async-done | bytes 2097184 | tf_op jit(solution)/shard_map/all_to_all | solution.py:298
  165.8 17.0 %shard_map.65 = bf16[32,4,16,512]{3,2,1,0:T(8,128)(2,1)S(1)} custom-call(s32[256,1]{1,0:T(8,128)S(1)} %broadcast_in_dim_tile.4.pos_ref, bf16[32,4,16,512]{3,2,1,0:T(8,128)(2,1)} %all-to-all-done.q_ref, bf16[2048,512]{1,0:T(8,128)(2,1)} %cache_ref.1), custom_call_target="tpu_custom_call" | custom-call | flops 8589934592 | bytes 6291456 | tf_op jit(solution)/shard_map/pallas_call | solution.py:236
  182.8 0.0 all-gather.3.cloned.1.call-done
  182.9 9.8 %shard_map.66 = bf16[16,16384]{1,0:T(8,128)(2,1)} custom-call(bf16[8,4,4,16,512]{4,3,2,1,0:T(8,128)(2,1)S(1)} %bitcast.4, bf16[8,4,32,64,128]{4,3,2,1,0:T(8,128)(2,1)} %bitcast.5), custom_call_target="tpu_custom_call" | custom-call | flops 268435456 | bytes 18874368 | tf_op jit(solution)/shard_map/pallas_call | solution.py:272
  (1 shorter events, 0.0 us)
Async XLA Ops:
  6.5 176.3 %all-gather.3.cloned.1.call-start = ((), (), s32[]{:S(2)}) async-start(), calls=%async_computation.1 | async-start | bytes 17301504 | tf_op jit(solution)/shard_map/all_gather | solution.py:295
  9.0 3.0 %copy-start = (bf16[16,1536]{1,0:T(8,128)(2,1)S(1)}, bf16[16,1536]{1,0:T(8,128)(2,1)}, u32[]{:S(2)}) copy-start(bf16[16,1536]{1,0:T(8,128)(2,1)} %queries_ref.1) | copy-start | bytes 147460
  71.9 4.4 %copy-start.1 = (s32[16]{0:T(128)S(1)}, s32[16]{0:T(128)}, u32[]{:S(2)}) copy-start(s32[16]{0:T(128)} %param.11) | copy-start | bytes 196
  71.9 93.9 %all-to-all-start = ((bf16[32,4,16,512]{3,2,1,0:T(8,128)(2,1)}), bf16[32,4,16,512]{3,2,1,0:T(8,128)(2,1)}, u32[]{:S(2)}, u32[]{:S(2)}) async-start(bf16[32,4,16,512]{3,2,1,0:T(8,128)(2,1)} %shard_map.64), calls=%async_computation | async-start | bytes 4194304 | tf_op jit(solution)/shard_map/all_to_all | solution.py:298
Sparse Core Ops, SparseCore 0:
  10.3 162.1 all-gather.2

commit v3 on v0

v3 whole, which is shorter than its diff:
```python
import functools

import jax
import jax.numpy as jnp
from jax import lax
from jax.experimental import pallas as pl
from jax.experimental.pallas import tpu as pltpu
from jax.sharding import PartitionSpec as P

score_scale = 192.0 ** (-0.5)
VMEM = 58 << 20


def body(n_fsdp, n_grp, q_cols, f_step, *refs):
    pos_ref, qk_ref, queries_ref, v_ref, cache_ref, out_ref = refs[:6]
    qk_all, rows_all, absorbed, q_send, q_recv, values, keys_all, latents = refs[6:14]
    (local_sem, qk_s, qk_r, grp_s, grp_r, far_s, far_r, pair_s, pair_r) = refs[14:23]
    (abs_s, abs_r, right_s, left_s, line_r) = refs[23:28]
    (b_s, a_s, ahead_s, aside_s, val_r, twin_s, twin_r) = refs[28:]
    f, g = lax.axis_index("fsdp"), lax.axis_index("grp")
    devices = n_fsdp * n_grp
    me = f * n_grp + g
    pairs = n_fsdp // 2
    n_a = pairs // 2
    chip, core = lax.div(f, 2), lax.rem(f, 2)
    a, b = lax.div(chip, 2), lax.rem(chip, 2)
    partner = chip * 2 + 1 - core
    b_peer = (a * 2 + 1 - b) * 2 + core
    own, rank = q_recv.shape[2], q_recv.shape[-1]
    rows = rows_all.shape[2]
    half_heads = values.shape[2] // 2
    hd = values.shape[-1]

    def send(src, dst, send_sem, recv_sem, to):
        return pltpu.make_async_remote_copy(
            src_ref=src,
            dst_ref=dst,
            send_sem=send_sem,
            recv_sem=recv_sem,
            device_id=to,
            device_id_type=pl.DeviceIdType.MESH,
        )

    barrier = pltpu.get_barrier_semaphore()

    @pl.loop(1, devices)
    def _(step):
        other = lax.rem(me + step, devices)
        pl.semaphore_signal(
            barrier,
            inc=1,
            device_id=(lax.div(other, n_grp), lax.rem(other, n_grp)),
            device_id_type=pl.DeviceIdType.MESH,
        )

    locals_ = [
        pltpu.make_async_copy(qk_ref.at[f], qk_all.at[f], local_sem.at[0]),
        pltpu.make_async_copy(queries_ref, rows_all.at[f, g], local_sem.at[1]),
        pltpu.make_async_copy(v_ref, values.at[f, g], local_sem.at[2]),
        pltpu.make_async_copy(cache_ref, keys_all, local_sem.at[3]),
    ]
    for copy in locals_:
        copy.start()
    pl.semaphore_wait(barrier, devices - 1)

    def grp_copy(peer, slot):
        return send(
            queries_ref, rows_all.at[f, slot], grp_s.at[peer], grp_r.at[slot], (f, peer)
        )

    def qk_copy(peer, slot):
        return send(qk_ref.at[peer], qk_all.at[slot], qk_s.at[peer], qk_r.at[slot], (peer, g))

    def far_copy(peer, slot):
        block = rows_all.at[slot]
        return send(block, block, far_s.at[peer], far_r.at[slot], (peer, g))

    def pair_copy(slot):
        block, k = rows_all.at[slot], lax.div(slot, 2)
        return send(block, block, pair_s.at[k], pair_r.at[k], (partner, g))

    def abs_copy(peer, slot):
        pf, pg = lax.div(peer, n_grp), lax.rem(peer, n_grp)
        sf, sg = lax.div(slot, n_grp), lax.rem(slot, n_grp)
        return send(q_send.at[pf, pg], q_recv.at[sf, sg], abs_s.at[peer], abs_r.at[slot], (pf, pg))

    def line_copy(src, slot, sems, to):
        return send(src, values.at[f, slot], sems.at[slot], line_r.at[slot], (f, to))

    def half(block, h):
        return values.at[block, :, pl.ds(h * half_heads, half_heads)]

    def val_copy(block, h, send_sem, to):
        return send(half(block, h), half(block, h), send_sem, val_r.at[block, h], (to, g))

    def twin_copy(block, h):
        k = lax.div(block, 2)
        return send(half(block, h), half(block, h), twin_s.at[k, h], twin_r.at[k, h], (partner, g))

    def a_peer(step):
        other = lax.rem(a + step, n_a)
        return other, (other * 2 + b) * 2 + core

    @pl.loop(1, n_grp)
    def _(step):
        grp_copy(lax.rem(g + step, n_grp), g).start()

    @pl.loop(1, n_fsdp)
    def _(step):
        qk_copy(lax.rem(f + step, n_fsdp), f).start()

    @pl.when(g < n_grp - 1)
    def _():
        line_copy(v_ref, g, right_s, g + 1).start()

    @pl.when(g > 0)
    def _():
        line_copy(v_ref, g, left_s, g - 1).start()

    locals_[1].wait()

    @pl.loop(1, n_grp)
    def _(step):
        other = lax.rem(g + step, n_grp)
        grp_copy(other, other).wait_recv()

    @pl.loop(1, pairs)
    def _(step):
        far_copy(lax.rem(chip + step, pairs) * 2 + core, f).start()

    pair_copy(f).start()

    @pl.loop(1, pairs)
    def _(step):
        other = lax.rem(chip + step, pairs) * 2 + core
        far_copy(other, other).wait_recv()
        pair_copy(other).start()

    def pass_on(k):
        @pl.when(g - k >= 0)
        def _():
            slot = g - k
            line_copy(values.at[f, slot], slot, right_s, g).wait_recv()

            @pl.when(g < n_grp - 1)
            def _():
                line_copy(values.at[f, slot], slot, right_s, g + 1).start()

        @pl.when(g + k < n_grp)
        def _():
            slot = g + k
            line_copy(values.at[f, slot], slot, left_s, g).wait_recv()

            @pl.when(g > 0)
            def _():
                line_copy(values.at[f, slot], slot, left_s, g - 1).start()

    for k in range(1, n_grp - 1):
        pass_on(k)

    locals_[0].wait()

    @pl.loop(1, n_fsdp)
    def _(step):
        other = lax.rem(f + step, n_fsdp)
        qk_copy(other, other).wait_recv()

    @pl.loop(0, own)
    def _(h):
        keys = jnp.concatenate([qk_all[s, h, :, q_cols:] for s in range(n_fsdp)], axis=-1)
        for s in range(n_fsdp):
            absorbed[h, s * q_cols : (s + 1) * q_cols, :] = lax.dot_general(
                qk_all[s, h, :, :q_cols],
                keys,
                (((0,), (0,)), ((), ())),
                preferred_element_type=jnp.float32,
            ).astype(jnp.bfloat16)

    @pl.loop(0, pairs)
    def _(step):
        pair_copy(step * 2 + 1 - core).wait_recv()

    @pl.loop(0, own)
    def _(h):
        block = rows_all[...].reshape(devices * rows, rows_all.shape[-1])
        q_abs = jnp.dot(block, absorbed[h], preferred_element_type=jnp.float32)
        q_send[:, :, h] = q_abs.astype(jnp.bfloat16).reshape(n_fsdp, n_grp, rows, rank)

    @pl.loop(1, devices)
    def _(step):
        abs_copy(lax.rem(me + step, devices), me).start()

    q_recv[f, g] = q_send[f, g]

    locals_[2].wait()
    pass_on(n_grp - 1)
    for h in range(2):
        val_copy(f, h, b_s.at[h], b_peer).start()
        twin_copy(f, h).start()

        @pl.loop(1, n_a)
        def _(step, h=h):
            other, peer = a_peer(step)
            val_copy(f, h, a_s.at[other, h], peer).start()

    locals_[3].wait()
    blocks = n_fsdp // f_step
    middle = (n_grp * blocks) // 2

    @pl.loop(0, n_grp * blocks)
    def _(step):
        sg = lax.rem(g + lax.div(step, blocks), n_grp)
        first = lax.rem(step, blocks) * f_step

        @pl.when(step == middle)
        def _():
            for h in range(2):
                val_copy(b_peer, h, b_s.at[h], b_peer).wait_recv()
                twin_copy(b_peer, h).start()

            @pl.loop(1, n_a)
            def _(hop):
                other, peer = a_peer(hop)
                val_copy(b_peer, 0, ahead_s.at[other], peer).start()

            @pl.loop(1, n_a)
            def _(hop):
                other, peer = a_peer(hop)
                for h in (1, 0):
                    val_copy(peer, h, a_s.at[other, h], peer).wait_recv()
                    twin_copy(peer, h).start()
                    if h == 1:
                        val_copy(peer, 1, aside_s.at[other], b_peer).start()

        @pl.loop(0, f_step)
        def _(j):
            src = (first + j) * n_grp + sg

            @pl.when(src != me)
            def _():
                abs_copy(src, src).wait_recv()

        q = q_recv[pl.ds(first, f_step), sg].reshape(f_step * own * rows, rank)
        entries = keys_all.shape[0]
        index = lax.broadcasted_iota(jnp.int32, (q.shape[0], entries), 1)
        scores = lax.dot_general(
            q, keys_all[...], (((1,), (1,)), ((), ())), preferred_element_type=jnp.float32
        )
        scores = jnp.where(index <= pos_ref[...], scores * score_scale, jnp.float32(-1e30))
        top = jnp.max(scores, axis=-1, keepdims=True)
        weights = jnp.exp(scores - top)
        total = jnp.sum(weights, axis=-1, keepdims=True)
        probs = (weights * (1.0 / total)).astype(jnp.bfloat16)
        latent = jnp.dot(probs, keys_all[...], preferred_element_type=jnp.float32)
        latents[pl.ds(first, f_step), sg] = latent.astype(jnp.bfloat16).reshape(
            f_step, own, rows, rank
        )

    @pl.loop(1, n_a)
    def _(hop):
        other, peer = a_peer(hop)
        diagonal = (other * 2 + 1 - b) * 2 + core
        for h in range(2):
            val_copy(diagonal, h, ahead_s.at[other], peer).wait_recv()
            twin_copy(diagonal, h).start()

    @pl.loop(0, pairs)
    def _(k):
        for h in range(2):
            twin_copy(k * 2 + 1 - core, h).wait_recv()

    heads = n_fsdp * own

    @pl.loop(0, devices)
    def _(step):
        sg, sf = lax.div(step, n_fsdp), lax.rem(step, n_fsdp)
        for i in range(own):
            h = sf * own + i
            column = pl.multiple_of((sg * heads + h) * hd, hd)
            out_ref[:, pl.ds(column, hd)] = jnp.dot(
                latents[sf, sg, i],
                values[:, sg, h].reshape(rank, hd),
                preferred_element_type=jnp.float32,
            ).astype(jnp.bfloat16)

    @pl.loop(1, n_grp)
    def _(step):
        grp_copy(lax.rem(g + step, n_grp), g).wait_send()

    @pl.loop(1, n_fsdp)
    def _(step):
        qk_copy(lax.rem(f + step, n_fsdp), f).wait_send()

    @pl.loop(1, pairs)
    def _(step):
        far_copy(lax.rem(chip + step, pairs) * 2 + core, f).wait_send()

    @pl.loop(0, pairs)
    def _(step):
        pair_copy(step * 2 + core).wait_send()
        for h in range(2):
            twin_copy(step * 2 + core, h).wait_send()

    @pl.loop(1, devices)
    def _(step):
        abs_copy(lax.rem(me + step, devices), me).wait_send()

    @pl.loop(0, n_grp)
    def _(slot):
        @pl.when(jnp.logical_and(slot <= g, g < n_grp - 1))
        def _():
            line_copy(values.at[f, slot], slot, right_s, g + 1).wait_send()

        @pl.when(jnp.logical_and(slot >= g, g > 0))
        def _():
            line_copy(values.at[f, slot], slot, left_s, g - 1).wait_send()

    for h in range(2):
        val_copy(f, h, b_s.at[h], b_peer).wait_send()

    @pl.loop(1, n_a)
    def _(hop):
        other, peer = a_peer(hop)
        for h in range(2):
            val_copy(f, h, a_s.at[other, h], peer).wait_send()
        val_copy(b_peer, 0, ahead_s.at[other], peer).wait_send()
        val_copy(peer, 1, aside_s.at[other], b_peer).wait_send()


def shards(n_fsdp, n_grp, q_up, k_up, v_up, queries, cache, positions):
    heads, hd, q_cols = q_up.shape
    own = heads // n_fsdp
    k_cols = k_up.shape[-1]
    rank = n_fsdp * k_cols
    rows, q_rank = queries.shape
    devices = n_fsdp * n_grp
    pairs = n_fsdp // 2
    n_a = pairs // 2
    f_step = max(1, min(n_fsdp, 16 // own))
    qk = jnp.concatenate([q_up, k_up], axis=-1).reshape(n_fsdp, own, hd, q_cols + k_cols)
    pos = jnp.tile(positions, f_step * own)[:, None]
    dma = pltpu.SemaphoreType.DMA
    bf16 = jnp.bfloat16
    anywhere = pl.BlockSpec(memory_space=pl.ANY)
    vmem = pl.BlockSpec(memory_space=pltpu.VMEM)
    exchange = (n_fsdp, n_grp, own, rows, rank)
    return pl.pallas_call(
        functools.partial(body, n_fsdp, n_grp, q_cols, f_step),
        out_shape=jax.ShapeDtypeStruct((rows, n_grp * heads * hd), bf16),
        in_specs=[vmem, anywhere, anywhere, anywhere, anywhere],
        out_specs=vmem,
        scratch_shapes=[
            pltpu.VMEM(qk.shape, bf16),
            pltpu.VMEM((n_fsdp, n_grp, rows, q_rank), bf16),
            pltpu.VMEM((own, q_rank, rank), bf16),
            pltpu.VMEM(exchange, bf16),
            pltpu.VMEM(exchange, bf16),
            pltpu.VMEM((n_fsdp, n_grp, heads, k_cols, hd), bf16),
            pltpu.VMEM(cache.shape, bf16),
            pltpu.VMEM(exchange, bf16),
            dma((4,)),
            dma((n_fsdp,)),
            dma((n_fsdp,)),
            dma((n_grp,)),
            dma((n_grp,)),
            dma((n_fsdp,)),
            dma((n_fsdp,)),
            dma((pairs,)),
            dma((pairs,)),
            dma((devices,)),
            dma((devices,)),
            dma((n_grp,)),
            dma((n_grp,)),
            dma((n_grp,)),
            dma((2,)),
            dma((n_a, 2)),
            dma((n_a,)),
            dma((n_a,)),
            dma((n_fsdp, 2)),
            dma((pairs, 2)),
            dma((pairs, 2)),
        ],
        compiler_params=pltpu.CompilerParams(
            vmem_limit_bytes=VMEM, collective_id=0, has_side_effects=True
        ),
    )(pos, qk, queries, jnp.swapaxes(v_up, 1, 2), cache)


def solution(mesh):
    placed = (
        P("grp", None, "fsdp"),
        P("grp", None, "fsdp"),
        P("grp", None, "fsdp"),
        P(("fsdp", "grp"), None),
        P(("fsdp", "grp"), None),
        P(("fsdp", "grp")),
    )
    return jax.shard_map(
        functools.partial(shards, mesh.shape["fsdp"], mesh.shape["grp"]),
        mesh=mesh,
        in_specs=placed,
        out_specs=P(("fsdp", "grp"), None),
        check_vma=False,
    )
```

time: 486 us -> 173 us (0.36)
  waiting for transfers between devices: 287 us -> 0 us
  Pallas kernels: 0 us -> 166 us
  blocking collectives: 90.9 us -> 0 us
  matrix products: 48.5 us -> 0 us
  other arithmetic: 19.2 us -> 1.75 us
  between operations: 13.5 us -> 0.03 us
  starting transfers between devices: 10.5 us -> 0 us
  local copies, waits for them, and re-layouts: 12.4 us -> 5.56 us
    all_gather x2 -> x0, waiting for transfers between devices: 220 us -> none  [the longest x1 220 us: shards(): lax.all_gather(own_blocks, 'fsdp', axis=0, tiled=True)]
    pallas_call x0 -> x1, Pallas kernels: none -> 166 us  [shards(): pl.pallas_call(functools.partial(body, n_fsdp, n_grp, q_cols, f_step), ou...]
    all_to_all x3 -> x0, blocking collectives: 79 us -> none  [the longest x1 49.7 us: shards(): lax.all_to_all(latent, 'grp', split_axis=1, concat_axis=0, tiled=True)]
    all_to_all x2 -> x0, waiting for transfers between devices: 66.6 us -> none  [the longest x1 47.1 us: shards(): lax.all_to_all(q_abs, 'grp', split_axis=0, concat_axis=1, tiled=True)]
    dot_general x5 -> x0, matrix products: 48.5 us -> none  [the longest x1 21.5 us: shards(): jnp.einsum('rq,hqk->rhk', group_rows, lax.all_gather(own_blocks, 'fsdp',...]
    sub x1 -> x0, other arithmetic: 19.1 us -> none  [attend(): weights = jnp.exp(scores - row_max)]
    all_gather x1 -> x0, blocking collectives: 11.9 us -> none  [shards(): group_rows = lax.all_gather(queries, 'grp', axis=0, tiled=True)]
    all_to_all x2 -> x0, starting transfers between devices: 10.3 us -> none  [the longest x1 5.86 us: shards(): lax.all_to_all(q_up, 'fsdp', split_axis=0, concat_axis=2, tiled=True)]
  transfers between devices with their start and end apart: 4 -> 0, of which waited for: 3 -> 0; matrix products, arithmetic and copies ran while one was open for 9% -> 0% of each run, Pallas kernels for 0% -> 0%
where the time goes in v3:
time: 173 us
  Pallas kernels  166 us (96%)
  local copies, waits for them, and re-layouts  5.56 us (3%)
  other arithmetic  1.75 us (1%)
    pallas_call x1, Pallas kernels, shards(): pl.pallas_call(functools.partial(body, n_fsdp, n_grp, q_cols, f_step), ou...  166 us

profile of v3, /device:TPU:3, one launch (start us, length us, event | category | flops | bytes accessed | tf_op | source)
XLA Modules:
  0.0 172.9 jit_solution(10045757342862700054)
XLA Ops:
  0.0 1.7 %pad_maximum_fusion = bf16[32,128,256]{1,2,0:T(8,128)(2,1)S(1)} fusion(bf16[32,128,64]{1,2,0:T(8,128)(2,1)} %param.7, bf16[32,128,192]{1,2,0:T(8,128)(2,1)} %param.6), kind=kLoop, calls=%fused_computation | loop fusion | flops 4194304 | bytes 4194304 | tf_op jit(solution)/shard_map/concatenate | solution.py:340
  1.8 0.0 copy-start
  1.8 2.9 %copy.8 = bf16[32,128,256]{2,1,0:T(8,128)(2,1)} copy(bf16[32,128,256]{1,2,0:T(8,128)(2,1)S(1)} %pad_maximum_fusion) | data formatting | bytes 4194304 | tf_op jit(solution)/shard_map/concatenate | solution.py:340
  4.7 0.0 copy-done
  4.7 0.8 broadcast_in_dim_tile.4.refs_0_
  5.5 165.5 %shard_map.64 = bf16[16,16384]{1,0:T(8,128)(2,1)} custom-call(s32[256,1]{1,0:T(8,128)} %broadcast_in_dim_tile.4.refs_0_, bf16[8,4,128,256]{3,2,1,0:T(8,128)(2,1)} %bitcast.2, bf16[16,1536]{1,0:T(8,128)(2,1)} %refs_2_.1, bf16[32,64,128]{2,1,0:T(8,128)(2,1)} %bitcast.3, bf16[2048,512]{1,0:T(8,128)(2,1)} %refs_4_.1), custom_call_target="tpu_custom_call" | custom-call | tf_op jit(solution)/shard_map/pallas_call | solution.py:347
  171.0 1.9 %copy.11 = bf16[16,16384]{1,0:T(8,128)(2,1)} copy(bf16[16,16384]{1,0:T(8,128)(2,1)} %shard_map.64) | data formatting | bytes 1048576
  (1 shorter events, 0.0 us)
Async XLA Ops:
  1.8 2.9 %copy-start = (s32[16]{0:T(128)S(1)}, s32[16]{0:T(128)}, u32[]{:S(2)}) copy-start(s32[16]{0:T(128)} %param.11) | copy-start | bytes 196

commit v4 on v3

--- a/solution.py
+++ b/solution.py
@@ -192,17 +192,6 @@
 
     q_recv[f, g] = q_send[f, g]
 
-    locals_[2].wait()
-    pass_on(n_grp - 1)
-    for h in range(2):
-        val_copy(f, h, b_s.at[h], b_peer).start()
-        twin_copy(f, h).start()
-
-        @pl.loop(1, n_a)
-        def _(step, h=h):
-            other, peer = a_peer(step)
-            val_copy(f, h, a_s.at[other, h], peer).start()
-
     locals_[3].wait()
     blocks = n_fsdp // f_step
     middle = (n_grp * blocks) // 2
@@ -211,6 +200,19 @@
     def _(step):
         sg = lax.rem(g + lax.div(step, blocks), n_grp)
         first = lax.rem(step, blocks) * f_step
+
+        @pl.when(step == blocks)
+        def _():
+            locals_[2].wait()
+            pass_on(n_grp - 1)
+            for h in range(2):
+                val_copy(f, h, b_s.at[h], b_peer).start()
+                twin_copy(f, h).start()
+
+                @pl.loop(1, n_a)
+                def _(step, h=h):
+                    other, peer = a_peer(step)
+                    val_copy(f, h, a_s.at[other, h], peer).start()
 
         @pl.when(step == middle)
         def _():

time: 173 us -> 179 us (1.035); the launches traced: 173 us -> 177 us
  Pallas kernels: 166 us -> 170 us
    pallas_call x1, Pallas kernels: 166 us -> 170 us  [shards(): pl.pallas_call(functools.partial(body, n_fsdp, n_grp, q_cols, f_step), ou...]
where the time goes in v4:
time: 179 us; the launch traced here: 177 us
  Pallas kernels  170 us (95%)
  local copies, waits for them, and re-layouts  5.56 us (3%)
    pallas_call x1, Pallas kernels, shards(): pl.pallas_call(functools.partial(body, n_fsdp, n_grp, q_cols, f_step), ou...  170 us

profile of v4, /device:TPU:3, one launch (start us, length us, event | category | flops | bytes accessed | tf_op | source)
XLA Modules:
  0.0 177.0 jit_solution(2527325446022961828)
XLA Ops:
  0.0 1.7 pad_maximum_fusion
  1.8 0.0 copy-start
  1.8 2.9 %copy.8 = bf16[32,128,256]{2,1,0:T(8,128)(2,1)} copy(bf16[32,128,256]{1,2,0:T(8,128)(2,1)S(1)} %pad_maximum_fusion) | data formatting | bytes 4194304 | tf_op jit(solution)/shard_map/concatenate | solution.py:342
  4.7 0.0 copy-done
  4.7 0.8 broadcast_in_dim_tile.4.refs_0_
  5.5 169.7 %shard_map.64 = bf16[16,16384]{1,0:T(8,128)(2,1)} custom-call(s32[256,1]{1,0:T(8,128)} %broadcast_in_dim_tile.4.refs_0_, bf16[8,4,128,256]{3,2,1,0:T(8,128)(2,1)} %bitcast.2, bf16[16,1536]{1,0:T(8,128)(2,1)} %refs_2_.1, bf16[32,64,128]{2,1,0:T(8,128)(2,1)} %bitcast.3, bf16[2048,512]{1,0:T(8,128)(2,1)} %refs_4_.1), custom_call_target="tpu_custom_call" | custom-call | tf_op jit(solution)/shard_map/pallas_call | solution.py:349
  175.1 1.9 %copy.11 = bf16[16,16384]{1,0:T(8,128)(2,1)} copy(bf16[16,16384]{1,0:T(8,128)(2,1)} %shard_map.64) | data formatting | bytes 1048576
  (1 shorter events, 0.0 us)
Async XLA Ops:
  1.8 2.9 %copy-start = (s32[16]{0:T(128)S(1)}, s32[16]{0:T(128)}, u32[]{:S(2)}) copy-start(s32[16]{0:T(128)} %param.11) | copy-start | bytes 196

commit v5 on v3

--- a/solution.py
+++ b/solution.py
@@ -196,12 +196,14 @@
     pass_on(n_grp - 1)
     for h in range(2):
         val_copy(f, h, b_s.at[h], b_peer).start()
-        twin_copy(f, h).start()
 
         @pl.loop(1, n_a)
-        def _(step, h=h):
+        def _(step, h=1 - h):
             other, peer = a_peer(step)
             val_copy(f, h, a_s.at[other, h], peer).start()
+
+    for h in range(2):
+        twin_copy(f, h).start()
 
     locals_[3].wait()
     blocks = n_fsdp // f_step

time: 173 us -> 173 us (level)
  no operation moved by 1% of the time
where the time goes in v5:
time: 173 us
  Pallas kernels  166 us (96%)
  local copies, waits for them, and re-layouts  5.56 us (3%)
  other arithmetic  1.75 us (1%)
    pallas_call x1, Pallas kernels, shards(): pl.pallas_call(functools.partial(body, n_fsdp, n_grp, q_cols, f_step), ou...  166 us

profile of v5, /device:TPU:3, one launch (start us, length us, event | category | flops | bytes accessed | tf_op | source)
XLA Modules:
  0.0 172.9 jit_solution(17688541563165178147)
XLA Ops:
  0.0 1.7 %pad_maximum_fusion = bf16[32,128,256]{1,2,0:T(8,128)(2,1)S(1)} fusion(bf16[32,128,64]{1,2,0:T(8,128)(2,1)} %param.7, bf16[32,128,192]{1,2,0:T(8,128)(2,1)} %param.6), kind=kLoop, calls=%fused_computation | loop fusion | flops 4194304 | bytes 4194304 | tf_op jit(solution)/shard_map/concatenate | solution.py:342
  1.8 0.0 copy-start
  1.8 2.9 %copy.8 = bf16[32,128,256]{2,1,0:T(8,128)(2,1)} copy(bf16[32,128,256]{1,2,0:T(8,128)(2,1)S(1)} %pad_maximum_fusion) | data formatting | bytes 4194304 | tf_op jit(solution)/shard_map/concatenate | solution.py:342
  4.7 0.0 copy-done
  4.7 0.8 broadcast_in_dim_tile.4.refs_0_
  5.5 165.5 %shard_map.64 = bf16[16,16384]{1,0:T(8,128)(2,1)} custom-call(s32[256,1]{1,0:T(8,128)} %broadcast_in_dim_tile.4.refs_0_, bf16[8,4,128,256]{3,2,1,0:T(8,128)(2,1)} %bitcast.2, bf16[16,1536]{1,0:T(8,128)(2,1)} %refs_2_.1, bf16[32,64,128]{2,1,0:T(8,128)(2,1)} %bitcast.3, bf16[2048,512]{1,0:T(8,128)(2,1)} %refs_4_.1), custom_call_target="tpu_custom_call" | custom-call | tf_op jit(solution)/shard_map/pallas_call | solution.py:349
  171.0 1.9 %copy.11 = bf16[16,16384]{1,0:T(8,128)(2,1)} copy(bf16[16,16384]{1,0:T(8,128)(2,1)} %shard_map.64) | data formatting | bytes 1048576
  (1 shorter events, 0.0 us)
Async XLA Ops:
  1.8 2.9 %copy-start = (s32[16]{0:T(128)S(1)}, s32[16]{0:T(128)}, u32[]{:S(2)}) copy-start(s32[16]{0:T(128)} %param.11) | copy-start | bytes 196
